TPU v7x, 32 devices: a whole 2x2x4 slice. The times are simulated.
32 devices in a mesh: row: 16 (over z, x, core), col: 2 (over y).
Axes of the slice: x: 2, y: 2, z: 4, core: 2. Of those that a mesh axis runs over, the one named last changes fastest.
Arguments:
- features: bfloat16 [128, 64, 384], P('row', 'col'), may hold values from -6 to 6
- depth_weight: float32 [7, 7, 384], replicated, may hold values from -0.875 to 0.875
- depth_bias: float32 [384], replicated, may hold values from -3 to 3
- norm_gain: float32 [384], replicated, may hold values from 0.25 to 1.75
- norm_bias: float32 [384], replicated, may hold values from -2 to 2
- expand_weight: bfloat16 [384, 1536], replicated, may hold values from -0.3125 to 0.3125
- expand_bias: float32 [1536], replicated, may hold values from -3 to 3
- shrink_weight: bfloat16 [1536, 384], replicated, may hold values from -0.15625 to 0.15625
- shrink_bias: float32 [384], replicated, may hold values from -3 to 3
- layer_scale: float32 [384], replicated, may hold values from 0.3 to 3
- key_weight: bfloat16 [384, 384], replicated, may hold values from -0.3125 to 0.3125
- value_weight: bfloat16 [384, 384], replicated, may hold values from -0.3125 to 0.3125
- queries: bfloat16 [64, 384], replicated, may hold values from -192 to 192
- class_weight: float32 [384, 16], replicated, may hold values from -0.109375 to 0.109375
- tissue: int32 [16, 8], P('row', 'col'), may hold values from 0 to 1, as said below
- slide_label: int32 [16], replicated, may hold values from 0 to 1
Outputs:
- block_out: bfloat16 [128, 64, 384], P('row', 'col')
- pooled: float32 [64, 384], replicated
- slide_loss: float32 [1], replicated
Inputs may be any that keep to these rules, and one draw needn't show every extreme that they name: 0 or 1; tissue[0, 0] is 1.
All inputs are finite; a program needn't handle non-finite values.
Results may differ from a plain program's by a relative error of at most 0.028.
The roundings to bfloat16 on the way count: a program that leaves them out, or rounds other values in their place, can miss the bound.
Values may be sent and summed in bfloat16 or wider, within the bound.
A program may use at most 128 MiB of HBM per device.

v0:
```python
import jax
import jax.numpy as jnp
from jax import lax
from jax.sharding import PartitionSpec as P

NH = 8
NQ = 64
TILE = 8


def with_halo(block, sides, width):
    for axis, dim in sides:
        count = lax.axis_size(axis)
        forward = [(i, i + 1) for i in range(count - 1)]
        backward = [(target, source) for source, target in forward]
        low = lax.ppermute(
            lax.slice_in_dim(block, block.shape[dim] - width, None, axis=dim), axis, forward
        )
        high = lax.ppermute(lax.slice_in_dim(block, 0, width, axis=dim), axis, backward)
        block = jnp.concatenate([low, block, high], axis=dim)
    return block


def merged_2(part, axis, combine):
    gathered = jax.tree.map(lambda a: lax.all_gather(a, axis), part)

    def take(source):
        return jax.tree.map(lambda a: lax.dynamic_index_in_dim(a, source, 0, False), gathered)

    return lax.fori_loop(
        1, lax.axis_size(axis), lambda source, state: combine(state, take(source)), take(0)
    )


def spread_heads(scale, width):
    return jnp.repeat(jnp.transpose(scale), width // scale.shape[0], axis=1)


def combine(first, second):
    peak = jnp.maximum(first[0], second[0])
    factor_one = jnp.exp(first[0] - peak)
    factor_two = jnp.exp(second[0] - peak)
    total = first[1] * factor_one + second[1] * factor_two
    width = first[2].shape[1]
    weighted = first[2] * spread_heads(factor_one, width) + second[2] * spread_heads(
        factor_two, width
    )
    return (peak, total, weighted)


def per_device(
    features,
    depth_weight,
    depth_bias,
    norm_gain,
    norm_bias,
    expand_weight,
    expand_bias,
    shrink_weight,
    shrink_bias,
    layer_scale,
    key_weight,
    value_weight,
    queries,
    class_weight,
    tissue,
    slide_label,
):
    rows, cols, width = features.shape
    padded = with_halo(features, (("row", 0), ("col", 1)), 3)
    conv = jnp.zeros((rows, cols, width), jnp.float32) + depth_bias
    for offset_row in range(7):
        for offset_col in range(7):
            conv = (
                conv
                + padded[offset_row : offset_row + rows, offset_col : offset_col + cols].astype(
                    jnp.float32
                )
                * depth_weight[offset_row, offset_col]
            )
    center = jnp.mean(conv, axis=-1, keepdims=True)
    variance = jnp.mean((conv - center) ** 2, axis=-1, keepdims=True)
    normed = ((conv - center) * lax.rsqrt(variance + 1e-06) * norm_gain + norm_bias).astype(
        jnp.bfloat16
    )
    count = rows * cols
    expanded = (
        jnp.dot(normed.reshape(count, width), expand_weight, preferred_element_type=jnp.float32)
        + expand_bias
    )
    hidden = jax.nn.gelu(expanded, approximate=False).astype(jnp.bfloat16)
    shrunk = jnp.dot(hidden, shrink_weight, preferred_element_type=jnp.float32) + shrink_bias
    block_flat = (features.reshape(count, width).astype(jnp.float32) + layer_scale * shrunk).astype(
        jnp.bfloat16
    )
    keys = jnp.dot(block_flat, key_weight, preferred_element_type=jnp.float32).astype(jnp.bfloat16)
    values = jnp.dot(block_flat, value_weight, preferred_element_type=jnp.float32).astype(
        jnp.bfloat16
    )
    live_cells = jnp.repeat(jnp.repeat(tissue, TILE, axis=0), TILE, axis=1).reshape(count) > 0
    size = width // NH
    scores = jnp.einsum(
        "qhd,nhd->hqn",
        queries.reshape(NQ, NH, size),
        keys.reshape(count, NH, size),
        preferred_element_type=jnp.float32,
    ) * size ** (-0.5)
    live = live_cells[None, None, :]
    scores = jnp.where(live, scores, -1e30)
    peak = jnp.max(scores, axis=2)
    weights = jnp.where(live, jnp.exp(scores - peak[:, :, None]), 0.0)
    total = jnp.sum(weights, axis=2)
    rounded = weights.astype(jnp.bfloat16)
    weighted = jnp.einsum(
        "hqn,nhd->qhd", rounded, values.reshape(count, NH, size), preferred_element_type=jnp.float32
    ).reshape(NQ, width)
    merged = merged_2((peak, total, weighted), ("row", "col"), combine)
    pooled = merged[2] / spread_heads(merged[1], width)
    logits = jnp.sum(jnp.dot(pooled, class_weight, precision=lax.Precision.HIGHEST), axis=0)
    slide_loss = jnp.sum(
        jax.nn.softplus(logits) - slide_label.astype(jnp.float32) * logits
    ).reshape(1)
    return (block_flat.reshape(rows, cols, width), pooled, slide_loss)


def solution(mesh):
    placed = (
        P("row", "col", None),
        P(),
        P(),
        P(),
        P(),
        P(),
        P(),
        P(),
        P(),
        P(),
        P(),
        P(),
        P(),
        P(),
        P("row", "col"),
        P(),
    )
    return jax.shard_map(
        per_device,
        mesh=mesh,
        in_specs=placed,
        out_specs=(P("row", "col", None), P(), P()),
        check_vma=False,
    )
```

profile of v0, /device:TPU:0, one launch (start us, length us, event | category | flops | bytes accessed | tf_op | source)
XLA Modules:
  0.0 235.7 jit_solution(16296607326346940511)
XLA Ops:
  7.3 1.0 fusion.133
  8.3 1.3 collective-permute-start.1
  9.6 3.0 %collective-permute-start = (bf16[3,32,384]{2,1,0:T(8,128)(2,1)S(1)}, bf16[3,32,384]{2,1,0:T(8,128)(2,1)S(1)}, u32[]{:S(2)}, u32[]{:S(2)}) collective-permute-start(bf16[3,32,384]{2,1,0:T(8,128)(2,1)S(1)} %get-tuple-element.273), channel_id=1, source_target_pairs={{0,2},{2,4},{4,6},{6,8},{8,10},{10,12},{12,14},{14,16},{16,18},{18... | collective-permute-start | bytes 221192 | tf_op jit(solution)/shard_map/ppermute | solution.py:16
  13.3 1.3 slice_reduce_fusion.47
  14.6 1.4 slice_reduce_fusion.48
  16.0 1.0 constant_dynamic-update-slice_fusion.3
  17.2 4.9 %collective-permute-start.2 = (bf16[14,3,384]{2,1,0:T(4,128)(2,1)S(1)}, bf16[14,3,384]{2,1,0:T(4,128)(2,1)S(1)}, u32[]{:S(2)}, u32[]{:S(2)}) collective-permute-start(bf16[14,3,384]{2,1,0:T(4,128)(2,1)S(1)} %get-tuple-element.267), channel_id=1, source_target_pairs={{0,1},{2,3},{4,5},{6,7},{8,9},{10,11},{12,13},{14,15},{16,17},{18,... | collective-permute-start | bytes 96776 | tf_op jit(solution)/shard_map/ppermute | solution.py:16
  22.1 1.3 collective-permute-start.3
  23.4 1.0 slice_reduce_fusion.46
  24.6 3.7 %collective-permute-done.3 = bf16[14,3,384]{2,1,0:T(4,128)(2,1)S(1)} collective-permute-done((bf16[14,3,384]{2,1,0:T(4,128)(2,1)S(1)}, bf16[14,3,384]{2,1,0:T(4,128)(2,1)S(1)}, u32[]{:S(2)}, u32[]{:S(2)}) %collective-permute-start.3) | collective-permute-done | bytes 32288 | tf_op jit(solution)/shard_map/ppermute | solution.py:19
  28.3 4.2 %fusion.131 = (f32[8,32]{1,0:T(8,128)S(1)}, f32[8,32,384]{2,1,0:T(8,128)S(1)}) fusion(f32[384]{0:T(512)S(1)} %get-tuple-element.243, bf16[14,3,384]{2,1,0:T(4,128)(2,1)S(1)} %collective-permute-done.3, bf16[14,32,384]{2,1,0:T(8,128)(2,1)S(1)} %get-tuple-element.277, f32[384]{0:T(512)S(1)} %get-tuple-element.244, f32[384]{0:T(512)S(1)} %get-tuple-element.197, ...), kind=kLoop, calls=%fused_computation.299 | loop fusion | flops 26935040 | bytes 2255872 | tf_op jit(solution)/shard_map/reduce_sum | solution.py:81
  33.0 5.5 %fusion.19 = bf16[256,384]{1,0:T(8,128)(2,1)S(1)} fusion(bf16[1536,384]{1,0:T(8,128)(2,1)S(1)} %copy-done, bf16[256,384]{1,0:T(8,128)(2,1)S(1)} %bitcast.69, bf16[384,1536]{1,0:T(8,128)(2,1)} %param.23, f32[1536]{0:T(1024)S(1)} %copy-done.11, f32[384]{0:T(512)S(1)} %copy-done.12, f32[384]{0:T(512)S(1)} %copy-done.13, bf16[256,384]{1,0:T(8,128)(2,1)S(1)} %bitcast.63), kind=kOutput, calls=%fused_computation.78 | convolution fusion | flops 630423552 | bytes 2958336 | tf_op jit(solution)/shard_map/dot_general | solution.py:92
  40.8 65.7 %all-gather = f32[256,64]{1,0:T(8,128)S(1)} all-gather(f32[8,64]{1,0:T(8,128)S(1)} %get-tuple-element.278), channel_id=2, replica_groups=mesh['row'=16,'col'=2] {'row','col'}, dimensions={0}, use_global_device_ids=true | all-gather | bytes 67584 | tf_op jit(solution)/shard_map/all_gather | solution.py:25
  106.8 65.3 %all-gather.1 = f32[256,64]{1,0:T(8,128)S(1)} all-gather(f32[8,64]{1,0:T(8,128)S(1)} %fusion.52), channel_id=3, replica_groups=mesh['row'=16,'col'=2] {'row','col'}, dimensions={0}, use_global_device_ids=true | all-gather | bytes 67584 | tf_op jit(solution)/shard_map/all_gather | solution.py:25
  173.1 54.4 %while.19 = (s32[]{:T(128)}, f32[8,64]{0,1:T(8,128)S(1)}, f32[8,64]{0,1:T(8,128)S(1)}, f32[64,384]{1,0:T(8,128)S(1)}, f32[32,8,64]{2,1,0:T(8,128)S(1)}, /*index=...) while((s32[]{:T(128)}, f32[8,64]{0,1:T(8,128)S(1)}, ...), condition=%wide.region_5.6_spmd, body=%wide.region_4.5_spmd.sunk | while | flops 77317 | bytes 1128591 | solution.py:30
  174.0 0.9 fusion.152
  175.7 0.9 fusion.152
  177.5 0.9 fusion.152
  179.2 0.9 fusion.152
  181.0 0.9 fusion.152
  182.7 0.9 fusion.152
  184.5 0.9 fusion.152
  186.2 0.9 fusion.152
  188.0 0.9 fusion.152
  189.8 0.9 fusion.152
  191.5 0.9 fusion.152
  193.3 0.9 fusion.152
  195.0 0.9 fusion.152
  196.8 0.9 fusion.152
  202.1 0.9 fusion.152
  217.9 0.9 fusion.152
  226.6 0.9 fusion.152
  (389 shorter events, 42.3 us)
Async XLA Ops:
  7.2 25.8 %copy-start = (bf16[1536,384]{1,0:T(8,128)(2,1)S(1)}, bf16[1536,384]{1,0:T(8,128)(2,1)}, u32[]{:S(2)}) copy-start(bf16[1536,384]{1,0:T(8,128)(2,1)} %param.25) | copy-start | bytes 3538948
  7.2 21.1 %copy-start.1 = (bf16[8,32,384]{2,1,0:T(8,128)(2,1)S(1)}, bf16[8,32,384]{2,1,0:T(8,128)(2,1)}, u32[]{:S(2)}) copy-start(bf16[8,32,384]{2,1,0:T(8,128)(2,1)} %param.18) | copy-start | bytes 589828
  7.2 17.3 %copy-start.6 = (bf16[64,384]{1,0:T(8,128)(2,1)S(1)}, bf16[64,384]{1,0:T(8,128)(2,1)}, u32[]{:S(2)}) copy-start(bf16[64,384]{1,0:T(8,128)(2,1)} %param.30) | copy-start | bytes 147460
  7.2 21.1 %copy-start.8 = (f32[384]{0:T(512)S(1)}, f32[384]{0:T(512)}, u32[]{:S(2)}) copy-start(f32[384]{0:T(512)} %param.20) | copy-start | bytes 4612
  7.2 165.0 %all-gather.4.cloned.1.call-start = ((), (), s32[]{:S(2)}) async-start(), calls=%async_computation | async-start | bytes 3244032 | tf_op jit(solution)/shard_map/all_gather | solution.py:25
  8.3 8.8 %collective-permute-start.1 = (bf16[3,32,384]{2,1,0:T(8,128)(2,1)S(1)}, bf16[3,32,384]{2,1,0:T(8,128)(2,1)S(1)}, u32[]{:S(2)}, u32[]{:S(2)}) collective-permute-start(bf16[3,32,384]{2,1,0:T(8,128)(2,1)S(1)} %get-tuple-element.272), channel_id=1, source_target_pairs={{2,0},{4,2},{6,4},{8,6},{10,8},{12,10},{14,12},{16,14},{18,16},{20... | collective-permute-start | bytes 221192 | tf_op jit(solution)/shard_map/ppermute | solution.py:19
  9.6 6.4 %collective-permute-start = (bf16[3,32,384]{2,1,0:T(8,128)(2,1)S(1)}, bf16[3,32,384]{2,1,0:T(8,128)(2,1)S(1)}, u32[]{:S(2)}, u32[]{:S(2)}) collective-permute-start(bf16[3,32,384]{2,1,0:T(8,128)(2,1)S(1)} %get-tuple-element.273), channel_id=1, source_target_pairs={{0,2},{2,4},{4,6},{6,8},{8,10},{10,12},{12,14},{14,16},{16,18},{18... | collective-permute-start | bytes 221192 | tf_op jit(solution)/shard_map/ppermute | solution.py:16
  17.1 15.6 %copy-start.9 = (f32[384]{0:T(512)S(1)}, f32[384]{0:T(512)}, u32[]{:S(2)}) copy-start(f32[384]{0:T(512)} %param.22) | copy-start | bytes 4612
  17.1 15.6 %copy-start.10 = (f32[384]{0:T(512)S(1)}, f32[384]{0:T(512)}, u32[]{:S(2)}) copy-start(f32[384]{0:T(512)} %param.21) | copy-start | bytes 4612
  17.2 7.5 %collective-permute-start.2 = (bf16[14,3,384]{2,1,0:T(4,128)(2,1)S(1)}, bf16[14,3,384]{2,1,0:T(4,128)(2,1)S(1)}, u32[]{:S(2)}, u32[]{:S(2)}) collective-permute-start(bf16[14,3,384]{2,1,0:T(4,128)(2,1)S(1)} %get-tuple-element.267), channel_id=1, source_target_pairs={{0,1},{2,3},{4,5},{6,7},{8,9},{10,11},{12,13},{14,15},{16,17},{18,... | collective-permute-start | bytes 96776 | tf_op jit(solution)/shard_map/ppermute | solution.py:16
  22.1 6.2 %collective-permute-start.3 = (bf16[14,3,384]{2,1,0:T(4,128)(2,1)S(1)}, bf16[14,3,384]{2,1,0:T(4,128)(2,1)S(1)}, u32[]{:S(2)}, u32[]{:S(2)}) collective-permute-start(bf16[14,3,384]{2,1,0:T(4,128)(2,1)S(1)} %get-tuple-element.268), channel_id=1, source_target_pairs={{1,0},{3,2},{5,4},{7,6},{9,8},{11,10},{13,12},{15,14},{17,16},{19,... | collective-permute-start | bytes 96776 | tf_op jit(solution)/shard_map/ppermute | solution.py:19
  28.3 4.6 %copy-start.11 = (f32[1536]{0:T(1024)S(1)}, f32[1536]{0:T(1024)}, u32[]{:S(2)}) copy-start(f32[1536]{0:T(1024)} %param.24) | copy-start | bytes 18436
  28.3 4.6 %copy-start.12 = (f32[384]{0:T(512)S(1)}, f32[384]{0:T(512)}, u32[]{:S(2)}) copy-start(f32[384]{0:T(512)} %param.26) | copy-start | bytes 4612
  28.3 4.7 %copy-start.13 = (f32[384]{0:T(512)S(1)}, f32[384]{0:T(512)}, u32[]{:S(2)}) copy-start(f32[384]{0:T(512)} %param.27) | copy-start | bytes 4612
  33.0 5.5 %copy-start.4 = (bf16[384,384]{1,0:T(8,128)(2,1)S(1)}, bf16[384,384]{1,0:T(8,128)(2,1)}, u32[]{:S(2)}) copy-start(bf16[384,384]{1,0:T(8,128)(2,1)} %param.29) | copy-start | bytes 884740
  33.0 5.9 %copy-start.5 = (bf16[384,384]{1,0:T(8,128)(2,1)S(1)}, bf16[384,384]{1,0:T(8,128)(2,1)}, u32[]{:S(2)}) copy-start(bf16[384,384]{1,0:T(8,128)(2,1)} %param.28) | copy-start | bytes 884740
  38.5 1.5 copy-start.2
  173.1 54.8 %copy-start.7 = (f32[384,16]{0,1:T(8,128)S(1)}, f32[384,16]{0,1:T(8,128)}, u32[]{:S(2)}) copy-start(f32[384,16]{0,1:T(8,128)} %param.31) | copy-start | bytes 73732
  173.1 55.1 %copy-start.14 = (s32[16]{0:T(128)S(1)}, s32[16]{0:T(128)}, u32[]{:S(2)}) copy-start(s32[16]{0:T(128)} %param.33) | copy-start | bytes 196
  227.9 1.0 copy-start.3
Sparse Core Ops, SparseCore 0:
  40.9 59.6 all-gather.3
where the time goes:
time: 237 us; the launch traced here: 236 us
  blocking collectives  131 us (55%)
  other arithmetic  36.8 us (16%)
  local copies, waits for them, and re-layouts  30 us (13%)
  between operations  14.4 us (6%)
  starting transfers between devices  10.5 us (4%)
  matrix products  6.96 us (3%)
  waiting for transfers between devices  3.69 us (2%)
  loops' own time  2.4 us (1%)
    all_gather x2, blocking collectives, merged_2(): gathered = jax.tree.map(lambda a: lax.all_gather(a, axis), part)  131 us
    add x31, other arithmetic, combine(): first[2] * spread_heads(factor_one, width)  29.3 us
    reshape x63, local copies, waits for them, and re-layouts, spread_heads(): return jnp.repeat(jnp.transpose(scale), width // scale.shape[0], axis=1)  8.39 us
    ppermute x2, starting transfers between devices, with_halo(): lax.ppermute(lax.slice_in_dim(block, block.shape[dim] - width, None, axis...  7.91 us
    broadcast_in_dim x63, local copies, waits for them, and re-layouts, spread_heads(): return jnp.repeat(jnp.transpose(scale), width // scale.shape[0], axis=1)  7.66 us
    dynamic_slice x95, local copies, waits for them, and re-layouts, take(): lax.dynamic_index_in_dim(a, source, 0, False)  5.5 us
    dot_general x1, matrix products, per_device(): jnp.dot(hidden, shrink_weight, preferred_element_type=jnp.float32)  5.47 us
  transfers between devices with their start and end apart: 5, of which 1 were waited for; matrix products, arithmetic and copies ran while one was open for 3% of the time, Pallas kernels for 0%

commit v1 on v0

v1 whole, which is shorter than its diff:
```python
import functools

import jax
import jax.numpy as jnp
from jax import lax
from jax.experimental import pallas as pl
from jax.experimental.pallas import tpu as pltpu
from jax.sharding import PartitionSpec as P

NH = 8
NQ = 64
TILE = 8
LANES = 128
GROUP_ROWS, GROUP_COLS = 4, 2
GROUP = GROUP_ROWS * GROUP_COLS
QROWS = NQ // GROUP
MESH = pl.DeviceIdType.MESH
SIDES = [(-1, 0), (1, 0), (0, -1), (0, 1), (-1, -1), (-1, 1), (1, -1), (1, 1)]


def lane_ids(rows, width):
    return lax.broadcasted_iota(jnp.int32, (rows, width), 1)


def spread(cols, first, width):
    rows = cols.shape[0]
    head = lane_ids(rows, width) // (width // NH)
    out = jnp.zeros((rows, width), jnp.float32)
    for h in range(NH):
        out = jnp.where(head == h, cols[:, first + h : first + h + 1], out)
    return out


def combine(ref, count, width):
    tails = [ref[s, :, width:] for s in range(count)]
    peak = functools.reduce(jnp.maximum, tails)
    weighted = jnp.zeros((QROWS, width), jnp.float32)
    total = jnp.zeros((QROWS, LANES), jnp.float32)
    for s in range(count):
        factor = jnp.exp(tails[s] - peak)
        total = total + pltpu.roll(factor, NH, 1) * tails[s]
        weighted = weighted + ref[s, :, :width] * spread(factor, 0, width)
    return weighted, jnp.where(lane_ids(QROWS, LANES) < NH, peak, total)


def kernel(
    n_row, n_col,
    feat, dw, db, gain, nbias, w1_hbm, b1, w2_hbm, b2, scale, wk_hbm, wv_hbm, queries, cw, tissue, label,
    block_ref, pooled_ref, loss_ref,
    w1, w2, wk, wv, pad, left_pad, right_pad, conv, qbig,
    stage_l, stage_r, halo_rows, halo_cols, halo_corners, msg, got_a, got_b, mine, pooled,
    w_sem, hs_sem, hr_sem, as_sem, ar_sem, bs_sem, br_sem, cs_sem, cr_sem,
):
    rows, cols, width = feat.shape
    count = rows * cols
    chunks = width // LANES
    row, col = lax.axis_index("row"), lax.axis_index("col")

    loads = [
        pltpu.make_async_copy(src, dst, w_sem.at[i])
        for i, (src, dst) in enumerate(((w1_hbm, w1), (w2_hbm, w2), (wk_hbm, wk), (wv_hbm, wv)))
    ]
    for load in loads:
        load.start()

    base_row, base_col = (row // GROUP_ROWS) * GROUP_ROWS, (col // GROUP_COLS) * GROUP_COLS
    place = (row - base_row) * GROUP_COLS + (col - base_col)
    over = n_col // GROUP_COLS
    n_far = (n_row // GROUP_ROWS) * over
    far = (row // GROUP_ROWS) * over + col // GROUP_COLS

    def near_peer(step):
        other = (place + step) % GROUP
        return other, (base_row + other // GROUP_COLS, base_col + other % GROUP_COLS)

    def far_peer(step):
        other = (far + step) % n_far
        return other, (
            (other // over) * GROUP_ROWS + place // GROUP_COLS,
            (other % over) * GROUP_COLS + place % GROUP_COLS,
        )

    def present(side):
        dr, dc = side
        ok = None
        for delta, at, size in ((dr, row, n_row), (dc, col, n_col)):
            if delta:
                here = at > 0 if delta < 0 else at < size - 1
                ok = here if ok is None else jnp.logical_and(ok, here)
        return ok

    barrier = pltpu.get_barrier_semaphore()
    for side in SIDES:
        @pl.when(present(side))
        def _(side=side):
            pl.semaphore_signal(
                barrier, inc=1, device_id=(row + side[0], col + side[1]), device_id_type=MESH
            )
    for step in range(1, GROUP):
        pl.semaphore_signal(barrier, inc=1, device_id=near_peer(step)[1], device_id_type=MESH)
    for step in range(1, n_far):
        pl.semaphore_signal(barrier, inc=1, device_id=far_peer(step)[1], device_id_type=MESH)

    stage_l[...] = feat[:, 0:8, :].astype(jnp.float32).reshape(rows * 8, width).astype(jnp.bfloat16)
    stage_r[...] = (
        feat[:, cols - 8 : cols, :].astype(jnp.float32).reshape(rows * 8, width).astype(jnp.bfloat16)
    )

    landing = {
        (-1, 0): halo_rows.at[0], (1, 0): halo_rows.at[1],
        (0, -1): halo_cols.at[0], (0, 1): halo_cols.at[1],
        (-1, -1): halo_corners.at[0], (-1, 1): halo_corners.at[1],
        (1, -1): halo_corners.at[2], (1, 1): halo_corners.at[3],
    }

    def halo_copy(side):
        dr, dc = side
        if dc == 0:
            src = feat.at[pl.ds(0, 3)] if dr < 0 else feat.at[pl.ds(rows - 3, 3)]
        else:
            src = stage_l if dc < 0 else stage_r
            if dr:
                src = src.at[pl.ds(0 if dr < 0 else rows * 8 - 32, 32)]
        return pltpu.make_async_remote_copy(
            src_ref=src,
            dst_ref=landing[(-dr, -dc)],
            send_sem=hs_sem.at[SIDES.index(side)],
            recv_sem=hr_sem.at[SIDES.index((-dr, -dc))],
            device_id=(row + dr, col + dc),
            device_id_type=MESH,
        )

    greeted = jnp.int32(GROUP - 1 + n_far - 1)
    for side in SIDES:
        greeted = greeted + present(side).astype(jnp.int32)
    pl.semaphore_wait(barrier, greeted)
    for side in SIDES:
        @pl.when(present(side))
        def _(side=side):
            halo_copy(side).start()

        @pl.when(jnp.logical_not(present(side)))
        def _(side=side):
            landing[side][...] = jnp.zeros(landing[side].shape, jnp.bfloat16)

    for c in range(chunks):
        lanes = slice(c * LANES, (c + 1) * LANES)
        pad[c, 3 : 3 + rows, 8 : 8 + cols, :] = feat[:, :, lanes].astype(jnp.float32)
    pad[:, 3 : 3 + rows, 0:8, :] = jnp.zeros((chunks, rows, 8, LANES), jnp.float32)
    pad[:, 3 : 3 + rows, 8 + cols :, :] = jnp.zeros((chunks, rows, 8, LANES), jnp.float32)

    def own_part(c, carry):
        at = pl.ds(pl.multiple_of(c * LANES, LANES), LANES)
        acc = [jnp.broadcast_to(db[:, at], (cols, LANES)) for _ in range(rows)]
        for b in range(7):
            taps = [dw[a, b : b + 1, at] for a in range(7)]
            for r in range(3, 3 + rows):
                window = pad[c, r, b + 5 : b + 5 + cols, :]
                for a in range(7):
                    if 0 <= r - a < rows:
                        acc[r - a] = acc[r - a] + window * taps[a]
        for i in range(rows):
            conv[c, i] = acc[i]
        return carry

    lax.fori_loop(0, chunks, own_part, 0)

    q32 = queries[...].astype(jnp.float32)
    head = lane_ids(NQ, width) // (width // NH)
    for h in range(NH):
        qbig[h * NQ : (h + 1) * NQ, :] = jnp.where(head == h, q32, 0.0).astype(jnp.bfloat16)

    for side in SIDES:
        @pl.when(present(side))
        def _(side=side):
            pltpu.make_async_remote_copy(
                src_ref=landing[side],
                dst_ref=landing[side],
                send_sem=hs_sem.at[SIDES.index(side)],
                recv_sem=hr_sem.at[SIDES.index(side)],
                device_id=(row + side[0], col + side[1]),
                device_id_type=MESH,
            ).wait_recv()

    for c in range(chunks):
        lanes = slice(c * LANES, (c + 1) * LANES)
        for end, first in ((0, 0), (1, 3 + rows)):
            pad[c, first : first + 3, 8 : 8 + cols, :] = halo_rows[end, :, :, lanes].astype(jnp.float32)
            for side in range(2):
                corner = halo_corners[end * 2 + side, :, lanes].astype(jnp.float32).reshape(4, 8, LANES)
                start = 0 if side == 0 else 8 + cols
                pad[c, first : first + 3, start : start + 8, :] = corner[1:4] if end == 0 else corner[0:3]
        left_pad[c, :, 0:8, :] = halo_cols[0, :, lanes].astype(jnp.float32).reshape(rows, 8, LANES)
        right_pad[c, :, 8:16, :] = halo_cols[1, :, lanes].astype(jnp.float32).reshape(rows, 8, LANES)
    left_pad[:, :, 8:16, :] = jnp.zeros((chunks, rows, 8, LANES), jnp.float32)
    right_pad[:, :, 0:8, :] = jnp.zeros((chunks, rows, 8, LANES), jnp.float32)

    def border_part(c, carry):
        at = pl.ds(pl.multiple_of(c * LANES, LANES), LANES)
        acc = [conv[c, i] for i in range(rows)]
        low = [jnp.zeros((8, LANES), jnp.float32) for _ in range(rows)]
        high = [jnp.zeros((8, LANES), jnp.float32) for _ in range(rows)]
        for b in range(7):
            taps = [dw[a, b : b + 1, at] for a in range(7)]
            for r in list(range(3)) + list(range(3 + rows, 6 + rows)):
                window = pad[c, r, b + 5 : b + 5 + cols, :]
                for a in range(7):
                    if 0 <= r - a < rows:
                        acc[r - a] = acc[r - a] + window * taps[a]
            if b != 3:
                side, edge, start = (low, left_pad, b + 5) if b < 3 else (high, right_pad, b - 3)
                for r in range(3, 3 + rows):
                    window = edge[c, r - 3, start : start + 8, :]
                    for a in range(7):
                        if 0 <= r - a < rows:
                            side[r - a] = side[r - a] + window * taps[a]
        for i in range(rows):
            conv[c, i] = acc[i]
            conv[c, i, 0:8, :] = conv[c, i, 0:8, :] + low[i]
            conv[c, i, cols - 8 : cols, :] = conv[c, i, cols - 8 : cols, :] + high[i]
        return carry

    lax.fori_loop(0, chunks, border_part, 0)

    full = jnp.concatenate([conv[c].reshape(count, LANES) for c in range(chunks)], axis=1)
    center = jnp.mean(full, axis=-1, keepdims=True)
    off = full - center
    variance = jnp.mean(off * off, axis=-1, keepdims=True)
    normed = (off * lax.rsqrt(variance + 1e-06) * gain[...] + nbias[...]).astype(jnp.bfloat16)

    loads[0].wait()
    loads[1].wait()
    hid = w1.shape[1]
    piece = 384
    shrunk = jnp.zeros((count, width), jnp.float32)
    for start in range(0, hid, piece):
        part = slice(start, start + piece)
        expanded = jnp.dot(normed, w1[:, part], preferred_element_type=jnp.float32) + b1[:, part]
        hidden = (0.5 * expanded * (1.0 + lax.erf(expanded * 0.5**0.5))).astype(jnp.bfloat16)
        shrunk = shrunk + jnp.dot(hidden, w2[part, :], preferred_element_type=jnp.float32)
    shrunk = shrunk + b2[...]
    inputs = feat[...].astype(jnp.float32).reshape(count, width)
    block = (inputs + scale[...] * shrunk).astype(jnp.bfloat16)
    block_ref[...] = block.reshape(rows, cols, width)

    loads[2].wait()
    loads[3].wait()
    keys = jnp.dot(block, wk[...], preferred_element_type=jnp.float32).astype(jnp.bfloat16)
    values = jnp.dot(block, wv[...], preferred_element_type=jnp.float32).astype(jnp.bfloat16)
    scores = lax.dot_general(
        qbig[...], keys, (((1,), (1,)), ((), ())), preferred_element_type=jnp.float32
    ) * (width // NH) ** (-0.5)
    cell = lane_ids(1, count)
    tile = (cell // cols) // TILE * (cols // TILE) + (cell % cols) // TILE
    alive = jnp.zeros((1, count), jnp.int32)
    for i in range(rows // TILE):
        for j in range(cols // TILE):
            alive = jnp.where(tile == i * (cols // TILE) + j, tissue[i, j], alive)
    live = alive > 0
    scores = jnp.where(live, scores, -1e30)
    peak = jnp.max(scores, axis=1, keepdims=True)
    weights = jnp.where(live, jnp.exp(scores - peak), 0.0)
    total = jnp.sum(weights, axis=1, keepdims=True)
    mixed = jnp.dot(weights.astype(jnp.bfloat16), values, preferred_element_type=jnp.float32)
    weighted = jnp.zeros((NQ, width), jnp.float32)
    tail = jnp.zeros((NQ, LANES), jnp.float32)
    lane = lane_ids(NQ, LANES)
    for h in range(NH):
        own = slice(h * NQ, (h + 1) * NQ)
        weighted = jnp.where(head == h, mixed[own], weighted)
        tail = jnp.where(lane == h, peak[own], tail)
        tail = jnp.where(lane == NH + h, total[own], tail)
    msg[:, :width] = weighted
    msg[:, width:] = tail

    copies_a = []
    for step in range(1, GROUP):
        other, device = near_peer(step)
        copies_a.append((other, pltpu.make_async_remote_copy(
            src_ref=msg.at[pl.ds(pl.multiple_of(other * QROWS, QROWS), QROWS)],
            dst_ref=got_a.at[place],
            send_sem=as_sem.at[step],
            recv_sem=ar_sem.at[place],
            device_id=device,
            device_id_type=MESH,
        )))
        copies_a[-1][1].start()
    got_a[place] = msg[pl.ds(pl.multiple_of(place * QROWS, QROWS), QROWS), :]

    def arrival(dst, sem):
        return pltpu.make_async_remote_copy(
            src_ref=dst, dst_ref=dst, send_sem=as_sem.at[0], recv_sem=sem,
            device_id=near_peer(1)[1], device_id_type=MESH,
        )

    for step in range(1, GROUP):
        other = near_peer(step)[0]
        arrival(got_a.at[other], ar_sem.at[other]).wait_recv()
    weighted, tail = combine(got_a, GROUP, width)

    if n_far > 1:
        mine[:, :width] = weighted
        mine[:, width:] = tail
        copies_b = []
        for step in range(1, n_far):
            other, device = far_peer(step)
            copies_b.append(pltpu.make_async_remote_copy(
                src_ref=mine,
                dst_ref=got_b.at[far],
                send_sem=bs_sem.at[step],
                recv_sem=br_sem.at[far],
                device_id=device,
                device_id_type=MESH,
            ))
            copies_b[-1].start()
        got_b[far] = mine[...]
        for step in range(1, n_far):
            other = far_peer(step)[0]
            arrival(got_b.at[other], br_sem.at[other]).wait_recv()
        weighted, tail = combine(got_b, n_far, width)
    pooled[place] = weighted / spread(tail, NH, width)

    copies_c = []
    for step in range(1, GROUP):
        other, device = near_peer(step)
        copies_c.append(pltpu.make_async_remote_copy(
            src_ref=pooled.at[place],
            dst_ref=pooled.at[place],
            send_sem=cs_sem.at[step],
            recv_sem=cr_sem.at[place],
            device_id=device,
            device_id_type=MESH,
        ))
        copies_c[-1].start()
    for step in range(1, GROUP):
        other = near_peer(step)[0]
        arrival(pooled.at[other], cr_sem.at[other]).wait_recv()
    result = pooled[...].reshape(NQ, width)
    pooled_ref[...] = result
    summed = jnp.sum(result, axis=0, keepdims=True)
    logits = jnp.dot(
        jnp.broadcast_to(summed, (8, width)), cw[...],
        precision=lax.Precision.HIGHEST, preferred_element_type=jnp.float32,
    )[0:1]
    soft = jnp.maximum(logits, 0.0) + jnp.log1p(jnp.exp(-jnp.abs(logits)))
    loss_ref[0] = jnp.sum(soft - label[...].astype(jnp.float32) * logits)

    for side in SIDES:
        @pl.when(present(side))
        def _(side=side):
            halo_copy(side).wait_send()
    for _, copy in copies_a:
        copy.wait_send()
    if n_far > 1:
        for copy in copies_b:
            copy.wait_send()
    for copy in copies_c:
        copy.wait_send()


def per_device(
    n_row, n_col,
    features, depth_weight, depth_bias, norm_gain, norm_bias, expand_weight, expand_bias,
    shrink_weight, shrink_bias, layer_scale, key_weight, value_weight, queries, class_weight,
    tissue, slide_label,
):
    rows, cols, width = features.shape
    hid = expand_weight.shape[1]
    chunks = width // LANES
    n_far = (n_row // GROUP_ROWS) * (n_col // GROUP_COLS)
    vmem = pl.BlockSpec(memory_space=pltpu.VMEM)
    smem = pl.BlockSpec(memory_space=pltpu.SMEM)
    hbm = pl.BlockSpec(memory_space=pl.ANY)
    wide = width + LANES
    f32, bf16 = jnp.float32, jnp.bfloat16
    dma = pltpu.SemaphoreType.DMA
    block, pooled, loss = pl.pallas_call(
        functools.partial(kernel, n_row, n_col),
        out_shape=(
            jax.ShapeDtypeStruct((rows, cols, width), bf16),
            jax.ShapeDtypeStruct((NQ, width), f32),
            jax.ShapeDtypeStruct((1,), f32),
        ),
        in_specs=[vmem, vmem, vmem, vmem, vmem, hbm, vmem, hbm, vmem, vmem, hbm, hbm, vmem, vmem, smem, vmem],
        out_specs=(vmem, vmem, smem),
        scratch_shapes=[
            pltpu.VMEM((width, hid), bf16),
            pltpu.VMEM((hid, width), bf16),
            pltpu.VMEM((width, width), bf16),
            pltpu.VMEM((width, width), bf16),
            pltpu.VMEM((chunks, rows + 6, cols + 16, LANES), f32),
            pltpu.VMEM((chunks, rows, 16, LANES), f32),
            pltpu.VMEM((chunks, rows, 16, LANES), f32),
            pltpu.VMEM((chunks, rows, cols, LANES), f32),
            pltpu.VMEM((NH * NQ, width), bf16),
            pltpu.VMEM((rows * 8, width), bf16),
            pltpu.VMEM((rows * 8, width), bf16),
            pltpu.VMEM((2, 3, cols, width), bf16),
            pltpu.VMEM((2, rows * 8, width), bf16),
            pltpu.VMEM((4, 32, width), bf16),
            pltpu.VMEM((NQ, wide), f32),
            pltpu.VMEM((GROUP, QROWS, wide), f32),
            pltpu.VMEM((n_far, QROWS, wide), f32),
            pltpu.VMEM((QROWS, wide), f32),
            pltpu.VMEM((GROUP, QROWS, width), f32),
            dma((4,)),
            dma((8,)),
            dma((8,)),
            dma((GROUP,)),
            dma((GROUP,)),
            dma((n_far,)),
            dma((n_far,)),
            dma((GROUP,)),
            dma((GROUP,)),
        ],
        compiler_params=pltpu.CompilerParams(
            collective_id=0, has_side_effects=True, vmem_limit_bytes=40 * 1024 * 1024
        ),
    )(
        features, depth_weight, depth_bias.reshape(1, width), norm_gain.reshape(1, width),
        norm_bias.reshape(1, width), expand_weight, expand_bias.reshape(1, hid), shrink_weight,
        shrink_bias.reshape(1, width), layer_scale.reshape(1, width), key_weight, value_weight,
        queries, class_weight, tissue, slide_label.reshape(1, -1),
    )
    return block, pooled, loss


def solution(mesh):
    everywhere = P()
    cells = P("row", "col", None)
    placed = (cells,) + (everywhere,) * 13 + (P("row", "col"), everywhere)
    return jax.shard_map(
        functools.partial(per_device, mesh.shape["row"], mesh.shape["col"]),
        mesh=mesh,
        in_specs=placed,
        out_specs=(cells, everywhere, everywhere),
        check_vma=False,
    )
```

time: 237 us -> 44.2 us (0.19)
  blocking collectives: 131 us -> 0 us
  other arithmetic: 36.8 us -> 0 us
  Pallas kernels: 0 us -> 26.5 us
  local copies, waits for them, and re-layouts: 30 us -> 14.7 us
  between operations: 14.4 us -> 2.42 us
  starting transfers between devices: 10.5 us -> 0 us
  matrix products: 6.96 us -> 0 us
  waiting for transfers between devices: 3.69 us -> 0 us
  loops' own time: 2.4 us -> 0 us
    all_gather x2 -> x0, blocking collectives: 131 us -> none  [merged_2(): gathered = jax.tree.map(lambda a: lax.all_gather(a, axis), part)]
    add x31 -> x0, other arithmetic: 29.3 us -> none  [combine(): first[2] * spread_heads(factor_one, width)]
    pallas_call x0 -> x1, Pallas kernels: none -> 26.5 us  [per_device(): pl.pallas_call(functools.partial(kernel, n_row, n_col), out_shape=(jax.Sh...]
    ppermute x4 -> x0, starting transfers between devices: 10.5 us -> none  [the longest x2 7.91 us: with_halo(): lax.ppermute(lax.slice_in_dim(block, block.shape[dim] - width, None, axis...]
    unnamed x31 -> x21, local copies, waits for them, and re-layouts: 0.1 us -> 10.6 us
    broadcast_in_dim x64 -> x0, local copies, waits for them, and re-layouts: 7.73 us -> none  [the longest x63 7.66 us: spread_heads(): return jnp.repeat(jnp.transpose(scale), width // scale.shape[0], axis=1)]
    dot_general x6 -> x0, matrix products: 6.96 us -> none  [the longest x1 5.47 us: per_device(): jnp.dot(hidden, shrink_weight, preferred_element_type=jnp.float32)]
    dynamic_slice x95 -> x0, local copies, waits for them, and re-layouts: 5.5 us -> none  [take(): lax.dynamic_index_in_dim(a, source, 0, False)]
  transfers between devices with their start and end apart: 5 -> 0, of which waited for: 1 -> 0; matrix products, arithmetic and copies ran while one was open for 3% -> 0% of each run, Pallas kernels for 0% -> 0%
where the time goes in v1:
time: 44.2 us; the launch traced here: 43.6 us
  Pallas kernels  26.5 us (60%)
  local copies, waits for them, and re-layouts  14.7 us (33%)
  between operations  2.42 us (5%)
    pallas_call x1, Pallas kernels, per_device(): pl.pallas_call(functools.partial(kernel, n_row, n_col), out_shape=(jax.Sh...  26.5 us
    unnamed x21, local copies, waits for them, and re-layouts  10.6 us

profile of v1, /device:TPU:0, one launch (start us, length us, event | category | flops | bytes accessed | tf_op | source)
XLA Modules:
  0.0 43.6 jit_solution(13862263082958943993)
XLA Ops:
  0.6 0.7 %reshape.27.db = f32[1,384]{1,0:T(1,128)S(1)} reshape(f32[384]{0:T(512)} %param.18) | data formatting | bytes 3072 | tf_op jit(solution)/shard_map/reshape | solution.py:420
  1.3 0.7 %reshape.28.gain = f32[1,384]{1,0:T(1,128)S(1)} reshape(f32[384]{0:T(512)} %param.19) | data formatting | bytes 3072 | tf_op jit(solution)/shard_map/reshape | solution.py:420
  2.0 0.7 %reshape.29.nbias = f32[1,384]{1,0:T(1,128)S(1)} reshape(f32[384]{0:T(512)} %param.20) | data formatting | bytes 3072 | tf_op jit(solution)/shard_map/reshape | solution.py:421
  2.7 0.7 %reshape.31.b2 = f32[1,384]{1,0:T(1,128)S(1)} reshape(f32[384]{0:T(512)} %param.24) | data formatting | bytes 3072 | tf_op jit(solution)/shard_map/reshape | solution.py:422
  3.4 0.7 %reshape.32.scale = f32[1,384]{1,0:T(1,128)S(1)} reshape(f32[384]{0:T(512)} %param.25) | data formatting | bytes 3072 | tf_op jit(solution)/shard_map/reshape | solution.py:422
  4.0 0.7 %reshape.30.b1 = f32[1,1536]{1,0:T(1,128)S(1)} reshape(f32[1536]{0:T(1024)} %param.22) | data formatting | bytes 12288 | tf_op jit(solution)/shard_map/reshape | solution.py:421
  4.7 0.9 %copy.19.cw = f32[384,16]{1,0:T(8,128)S(1)} copy(f32[384,16]{0,1:T(8,128)} %param.29) | data formatting | bytes 49152 | tf_op args[13]
  5.6 0.0 copy-start
  5.6 1.3 %copy-done = bf16[384,1536]{1,0:T(8,128)(2,1)S(1)} copy-done((bf16[384,1536]{1,0:T(8,128)(2,1)S(1)}, bf16[384,1536]{1,0:T(8,128)(2,1)}, u32[]{:S(2)}) %copy-start) | copy-done | bytes 1179672
  6.9 0.0 copy-start.1
  6.9 1.3 %copy-done.1 = bf16[1536,384]{1,0:T(8,128)(2,1)S(1)} copy-done((bf16[1536,384]{1,0:T(8,128)(2,1)S(1)}, bf16[1536,384]{1,0:T(8,128)(2,1)}, u32[]{:S(2)}) %copy-start.1) | copy-done | bytes 1179672
  8.2 0.0 copy-start.2
  8.2 1.0 %copy-done.2 = bf16[384,384]{1,0:T(8,128)(2,1)S(1)} copy-done((bf16[384,384]{1,0:T(8,128)(2,1)S(1)}, bf16[384,384]{1,0:T(8,128)(2,1)}, u32[]{:S(2)}) %copy-start.2) | copy-done | bytes 294936
  9.1 0.0 copy-start.3
  9.1 1.0 %copy-done.3 = bf16[384,384]{1,0:T(8,128)(2,1)S(1)} copy-done((bf16[384,384]{1,0:T(8,128)(2,1)S(1)}, bf16[384,384]{1,0:T(8,128)(2,1)}, u32[]{:S(2)}) %copy-start.3) | copy-done | bytes 294936
  10.1 0.0 copy-start.4
  10.1 0.9 %copy-done.4 = bf16[8,32,384]{2,1,0:T(8,128)(2,1)S(1)} copy-done((bf16[8,32,384]{2,1,0:T(8,128)(2,1)S(1)}, bf16[8,32,384]{2,1,0:T(8,128)(2,1)}, u32[]{:S(2)}) %copy-start.4) | copy-done | bytes 196632
  11.0 0.0 copy-start.5
  11.0 0.9 %copy-done.5 = f32[7,7,384]{2,1,0:T(8,128)S(1)} copy-done((f32[7,7,384]{2,1,0:T(8,128)S(1)}, f32[7,7,384]{2,1,0:T(8,128)}, u32[]{:S(2)}) %copy-start.5) | copy-done | bytes 75288
  11.9 0.0 copy-start.6
  11.9 0.8 %copy-done.6 = bf16[64,384]{1,0:T(8,128)(2,1)S(1)} copy-done((bf16[64,384]{1,0:T(8,128)(2,1)S(1)}, bf16[64,384]{1,0:T(8,128)(2,1)}, u32[]{:S(2)}) %copy-start.6) | copy-done | bytes 49176
  12.7 0.0 copy-start.7
  12.7 0.7 %copy-done.7 = s32[1,4]{1,0:T(1,128)S(1)} copy-done((s32[1,4]{1,0:T(1,128)S(1)}, s32[1,4]{1,0:T(1,128)}, u32[]{:S(2)}) %copy-start.7) | copy-done | bytes 40
  13.4 0.0 copy-start.8
  13.4 0.7 %copy-done.8 = s32[16]{0:T(128)S(1)} copy-done((s32[16]{0:T(128)S(1)}, s32[16]{0:T(128)}, u32[]{:S(2)}) %copy-start.8) | copy-done | bytes 88
  14.0 26.5 %shard_map.175 = (bf16[8,32,384]{2,1,0:T(8,128)(2,1)S(1)}, f32[64,384]{1,0:T(8,128)S(1)}, f32[1]{0:T(128)}) custom-call(bf16[8,32,384]{2,1,0:T(8,128)(2,1)S(1)} %copy-done.4, f32[7,7,384]{2,1,0:T(8,128)S(1)} %copy-done.5, f32[1,384]{1,0:T(1,128)S(1)} %reshape.27.db, f32[1,384]{1,0:T(1,128)S(1)} %reshape.28.gain, f32[1,384]{1,0:T(1,128)S(1)} %reshape.29.nbias, ...), custom_call_target="tpu_custom_call" | custom-call | tf_op jit(solution)/shard_map/pallas_call | solution.py:377
  40.5 0.7 %copy.23 = bf16[8,32,384]{2,1,0:T(8,128)(2,1)} copy(bf16[8,32,384]{2,1,0:T(8,128)(2,1)S(1)} %get-tuple-element.6) | data formatting | bytes 393216
  41.2 0.6 %copy.24 = f32[64,384]{1,0:T(8,128)} copy(f32[64,384]{1,0:T(8,128)S(1)} %get-tuple-element.7) | data formatting | bytes 196608
Async XLA Ops:
  5.6 1.3 %copy-start = (bf16[384,1536]{1,0:T(8,128)(2,1)S(1)}, bf16[384,1536]{1,0:T(8,128)(2,1)}, u32[]{:S(2)}) copy-start(bf16[384,1536]{1,0:T(8,128)(2,1)} %w1_hbm.1) | copy-start | bytes 3538948
  6.9 1.3 %copy-start.1 = (bf16[1536,384]{1,0:T(8,128)(2,1)S(1)}, bf16[1536,384]{1,0:T(8,128)(2,1)}, u32[]{:S(2)}) copy-start(bf16[1536,384]{1,0:T(8,128)(2,1)} %w2_hbm.1) | copy-start | bytes 3538948
  8.2 1.0 %copy-start.2 = (bf16[384,384]{1,0:T(8,128)(2,1)S(1)}, bf16[384,384]{1,0:T(8,128)(2,1)}, u32[]{:S(2)}) copy-start(bf16[384,384]{1,0:T(8,128)(2,1)} %wk_hbm.1) | copy-start | bytes 884740
  9.1 1.0 %copy-start.3 = (bf16[384,384]{1,0:T(8,128)(2,1)S(1)}, bf16[384,384]{1,0:T(8,128)(2,1)}, u32[]{:S(2)}) copy-start(bf16[384,384]{1,0:T(8,128)(2,1)} %wv_hbm.1) | copy-start | bytes 884740
  10.1 0.9 %copy-start.4 = (bf16[8,32,384]{2,1,0:T(8,128)(2,1)S(1)}, bf16[8,32,384]{2,1,0:T(8,128)(2,1)}, u32[]{:S(2)}) copy-start(bf16[8,32,384]{2,1,0:T(8,128)(2,1)} %feat.1) | copy-start | bytes 589828
  11.0 0.9 %copy-start.5 = (f32[7,7,384]{2,1,0:T(8,128)S(1)}, f32[7,7,384]{2,1,0:T(8,128)}, u32[]{:S(2)}) copy-start(f32[7,7,384]{2,1,0:T(8,128)} %dw.1) | copy-start | bytes 225796
  11.9 0.8 %copy-start.6 = (bf16[64,384]{1,0:T(8,128)(2,1)S(1)}, bf16[64,384]{1,0:T(8,128)(2,1)}, u32[]{:S(2)}) copy-start(bf16[64,384]{1,0:T(8,128)(2,1)} %queries.1) | copy-start | bytes 147460
  12.7 0.7 %copy-start.7 = (s32[1,4]{1,0:T(1,128)S(1)}, s32[1,4]{1,0:T(1,128)}, u32[]{:S(2)}) copy-start(s32[1,4]{1,0:T(1,128)} %tissue.1) | copy-start | bytes 52
  13.4 0.7 %copy-start.8 = (s32[16]{0:T(128)S(1)}, s32[16]{0:T(128)}, u32[]{:S(2)}) copy-start(s32[16]{0:T(128)} %param.31) | copy-start | bytes 196

commit v2 on v1

--- a/solution.py
+++ b/solution.py
@@ -14,6 +14,8 @@
 GROUP_ROWS, GROUP_COLS = 4, 2
 GROUP = GROUP_ROWS * GROUP_COLS
 QROWS = NQ // GROUP
+ORDER = (4, 5, 6, 7, 1, 2, 3, 0)
+CALLS = 2
 MESH = pl.DeviceIdType.MESH
 SIDES = [(-1, 0), (1, 0), (0, -1), (0, 1), (-1, -1), (-1, 1), (1, -1), (1, 1)]
 
@@ -45,21 +47,26 @@
 
 def kernel(
     n_row, n_col,
-    feat, dw, db, gain, nbias, w1_hbm, b1, w2_hbm, b2, scale, wk_hbm, wv_hbm, queries, cw, tissue, label,
+    feat_hbm, dw_hbm, db_hbm, gain_hbm, nbias_hbm, w1_hbm, b1_hbm, w2_hbm, b2_hbm, scale_hbm,
+    wk_hbm, wv_hbm, queries_hbm, cw_hbm, tissue_hbm, label_hbm,
     block_ref, pooled_ref, loss_ref,
-    w1, w2, wk, wv, pad, left_pad, right_pad, conv, qbig,
+    feat, dw, db, gain, nbias, w1, b1, w2, b2, scale, wkv, queries, cw, tissue, label, q32, pad, left_pad, right_pad, conv, qbig,
     stage_l, stage_r, halo_rows, halo_cols, halo_corners, msg, got_a, got_b, mine, pooled,
     w_sem, hs_sem, hr_sem, as_sem, ar_sem, bs_sem, br_sem, cs_sem, cr_sem,
 ):
-    rows, cols, width = feat.shape
+    rows, cols, width = feat_hbm.shape
     count = rows * cols
     chunks = width // LANES
     row, col = lax.axis_index("row"), lax.axis_index("col")
 
-    loads = [
-        pltpu.make_async_copy(src, dst, w_sem.at[i])
-        for i, (src, dst) in enumerate(((w1_hbm, w1), (w2_hbm, w2), (wk_hbm, wk), (wv_hbm, wv)))
-    ]
+    sources = (
+        (feat_hbm, feat), (dw_hbm, dw), (db_hbm, db), (queries_hbm, queries), (gain_hbm, gain),
+        (nbias_hbm, nbias), (w1_hbm, w1), (b1_hbm, b1), (w2_hbm, w2), (b2_hbm, b2),
+        (scale_hbm, scale), (wk_hbm, wkv.at[:, pl.ds(0, width)]),
+        (wv_hbm, wkv.at[:, pl.ds(width, width)]), (cw_hbm, cw), (tissue_hbm, tissue),
+        (label_hbm, label),
+    )
+    loads = [pltpu.make_async_copy(src, dst, w_sem.at[i]) for i, (src, dst) in enumerate(sources)]
     for load in loads:
         load.start()
 
@@ -101,6 +108,7 @@
     for step in range(1, n_far):
         pl.semaphore_signal(barrier, inc=1, device_id=far_peer(step)[1], device_id_type=MESH)
 
+    loads[0].wait()
     stage_l[...] = feat[:, 0:8, :].astype(jnp.float32).reshape(rows * 8, width).astype(jnp.bfloat16)
     stage_r[...] = (
         feat[:, cols - 8 : cols, :].astype(jnp.float32).reshape(rows * 8, width).astype(jnp.bfloat16)
@@ -149,9 +157,12 @@
     pad[:, 3 : 3 + rows, 0:8, :] = jnp.zeros((chunks, rows, 8, LANES), jnp.float32)
     pad[:, 3 : 3 + rows, 8 + cols :, :] = jnp.zeros((chunks, rows, 8, LANES), jnp.float32)
 
+    loads[1].wait()
+    loads[2].wait()
+
     def own_part(c, carry):
         at = pl.ds(pl.multiple_of(c * LANES, LANES), LANES)
-        acc = [jnp.broadcast_to(db[:, at], (cols, LANES)) for _ in range(rows)]
+        acc = [jnp.broadcast_to(db[at].reshape(1, LANES), (cols, LANES)) for _ in range(rows)]
         for b in range(7):
             taps = [dw[a, b : b + 1, at] for a in range(7)]
             for r in range(3, 3 + rows):
@@ -165,10 +176,14 @@
 
     lax.fori_loop(0, chunks, own_part, 0)
 
-    q32 = queries[...].astype(jnp.float32)
-    head = lane_ids(NQ, width) // (width // NH)
-    for h in range(NH):
-        qbig[h * NQ : (h + 1) * NQ, :] = jnp.where(head == h, q32, 0.0).astype(jnp.bfloat16)
+    loads[3].wait()
+    q32[...] = queries[...].astype(jnp.float32)
+    head = lane_ids(QROWS, width) // (width // NH)
+    for at, step in enumerate(ORDER):
+        other = near_peer(step)[0] if step else place
+        some = q32[pl.ds(pl.multiple_of(other * QROWS, QROWS), QROWS), :]
+        heads = [jnp.where(head == h, some, 0.0) for h in range(NH)]
+        qbig[at * NH * QROWS : (at + 1) * NH * QROWS, :] = jnp.concatenate(heads, axis=0).astype(jnp.bfloat16)
 
     for side in SIDES:
         @pl.when(present(side))
@@ -226,30 +241,29 @@
     center = jnp.mean(full, axis=-1, keepdims=True)
     off = full - center
     variance = jnp.mean(off * off, axis=-1, keepdims=True)
-    normed = (off * lax.rsqrt(variance + 1e-06) * gain[...] + nbias[...]).astype(jnp.bfloat16)
-
-    loads[0].wait()
-    loads[1].wait()
+    for load in loads[4:11]:
+        load.wait()
+    normed = (
+        off * lax.rsqrt(variance + 1e-06) * gain[...].reshape(1, width) + nbias[...].reshape(1, width)
+    ).astype(jnp.bfloat16)
+
     hid = w1.shape[1]
     piece = 384
     shrunk = jnp.zeros((count, width), jnp.float32)
     for start in range(0, hid, piece):
         part = slice(start, start + piece)
-        expanded = jnp.dot(normed, w1[:, part], preferred_element_type=jnp.float32) + b1[:, part]
+        expanded = jnp.dot(normed, w1[:, part], preferred_element_type=jnp.float32) + b1[part].reshape(1, piece)
         hidden = (0.5 * expanded * (1.0 + lax.erf(expanded * 0.5**0.5))).astype(jnp.bfloat16)
         shrunk = shrunk + jnp.dot(hidden, w2[part, :], preferred_element_type=jnp.float32)
-    shrunk = shrunk + b2[...]
+    shrunk = shrunk + b2[...].reshape(1, width)
     inputs = feat[...].astype(jnp.float32).reshape(count, width)
-    block = (inputs + scale[...] * shrunk).astype(jnp.bfloat16)
+    block = (inputs + scale[...].reshape(1, width) * shrunk).astype(jnp.bfloat16)
     block_ref[...] = block.reshape(rows, cols, width)
 
-    loads[2].wait()
-    loads[3].wait()
-    keys = jnp.dot(block, wk[...], preferred_element_type=jnp.float32).astype(jnp.bfloat16)
-    values = jnp.dot(block, wv[...], preferred_element_type=jnp.float32).astype(jnp.bfloat16)
-    scores = lax.dot_general(
-        qbig[...], keys, (((1,), (1,)), ((), ())), preferred_element_type=jnp.float32
-    ) * (width // NH) ** (-0.5)
+    for load in loads[11:]:
+        load.wait()
+    both = jnp.dot(block, wkv[...], preferred_element_type=jnp.float32).astype(jnp.bfloat16)
+    keys, values = both[:, :width], both[:, width:]
     cell = lane_ids(1, count)
     tile = (cell // cols) // TILE * (cols // TILE) + (cell % cols) // TILE
     alive = jnp.zeros((1, count), jnp.int32)
@@ -257,35 +271,45 @@
         for j in range(cols // TILE):
             alive = jnp.where(tile == i * (cols // TILE) + j, tissue[i, j], alive)
     live = alive > 0
-    scores = jnp.where(live, scores, -1e30)
-    peak = jnp.max(scores, axis=1, keepdims=True)
-    weights = jnp.where(live, jnp.exp(scores - peak), 0.0)
-    total = jnp.sum(weights, axis=1, keepdims=True)
-    mixed = jnp.dot(weights.astype(jnp.bfloat16), values, preferred_element_type=jnp.float32)
-    weighted = jnp.zeros((NQ, width), jnp.float32)
-    tail = jnp.zeros((NQ, LANES), jnp.float32)
-    lane = lane_ids(NQ, LANES)
-    for h in range(NH):
-        own = slice(h * NQ, (h + 1) * NQ)
-        weighted = jnp.where(head == h, mixed[own], weighted)
-        tail = jnp.where(lane == h, peak[own], tail)
-        tail = jnp.where(lane == NH + h, total[own], tail)
-    msg[:, :width] = weighted
-    msg[:, width:] = tail
-
+    lane = lane_ids(QROWS, LANES)
     copies_a = []
-    for step in range(1, GROUP):
-        other, device = near_peer(step)
-        copies_a.append((other, pltpu.make_async_remote_copy(
-            src_ref=msg.at[pl.ds(pl.multiple_of(other * QROWS, QROWS), QROWS)],
-            dst_ref=got_a.at[place],
-            send_sem=as_sem.at[step],
-            recv_sem=ar_sem.at[place],
-            device_id=device,
-            device_id_type=MESH,
-        )))
-        copies_a[-1][1].start()
-    got_a[place] = msg[pl.ds(pl.multiple_of(place * QROWS, QROWS), QROWS), :]
+    per_call = GROUP // CALLS
+    size = NH * QROWS
+    for call in range(CALLS):
+        scores = lax.dot_general(
+            qbig[call * per_call * size : (call + 1) * per_call * size, :], keys,
+            (((1,), (1,)), ((), ())), preferred_element_type=jnp.float32,
+        ) * (width // NH) ** (-0.5)
+        scores = jnp.where(live, scores, -1e30)
+        peak = jnp.max(scores, axis=1, keepdims=True)
+        weights = jnp.where(live, jnp.exp(scores - peak), 0.0)
+        total = jnp.sum(weights, axis=1, keepdims=True)
+        mixed = jnp.dot(weights.astype(jnp.bfloat16), values, preferred_element_type=jnp.float32)
+        for i in range(per_call):
+            at = call * per_call + i
+            weighted = jnp.zeros((QROWS, width), jnp.float32)
+            tail = jnp.zeros((QROWS, LANES), jnp.float32)
+            for h in range(NH):
+                own = slice(i * size + h * QROWS, i * size + (h + 1) * QROWS)
+                weighted = jnp.where(head == h, mixed[own], weighted)
+                tail = jnp.where(lane == h, peak[own], tail)
+                tail = jnp.where(lane == NH + h, total[own], tail)
+            step = ORDER[at]
+            if step == 0:
+                got_a[place, :, :width] = weighted
+                got_a[place, :, width:] = tail
+                continue
+            msg[at, :, :width] = weighted
+            msg[at, :, width:] = tail
+            copies_a.append(pltpu.make_async_remote_copy(
+                src_ref=msg.at[at],
+                dst_ref=got_a.at[place],
+                send_sem=as_sem.at[step],
+                recv_sem=ar_sem.at[place],
+                device_id=near_peer(step)[1],
+                device_id_type=MESH,
+            ))
+            copies_a[-1].start()
 
     def arrival(dst, sem):
         return pltpu.make_async_remote_copy(
@@ -338,18 +362,20 @@
     result = pooled[...].reshape(NQ, width)
     pooled_ref[...] = result
     summed = jnp.sum(result, axis=0, keepdims=True)
-    logits = jnp.dot(
-        jnp.broadcast_to(summed, (8, width)), cw[...],
-        precision=lax.Precision.HIGHEST, preferred_element_type=jnp.float32,
-    )[0:1]
+    logits = jnp.sum(summed * cw[...], axis=1, keepdims=True)
     soft = jnp.maximum(logits, 0.0) + jnp.log1p(jnp.exp(-jnp.abs(logits)))
-    loss_ref[0] = jnp.sum(soft - label[...].astype(jnp.float32) * logits)
+    n_lab = cw.shape[0]
+    which = lax.broadcasted_iota(jnp.int32, (n_lab, 1), 0)
+    truth = jnp.zeros((n_lab, 1), jnp.int32)
+    for k in range(n_lab):
+        truth = jnp.where(which == k, label[k], truth)
+    loss_ref[0] = jnp.sum(soft - truth.astype(jnp.float32) * logits)
 
     for side in SIDES:
         @pl.when(present(side))
         def _(side=side):
             halo_copy(side).wait_send()
-    for _, copy in copies_a:
+    for copy in copies_a:
         copy.wait_send()
     if n_far > 1:
         for copy in copies_b:
@@ -370,7 +396,7 @@
     n_far = (n_row // GROUP_ROWS) * (n_col // GROUP_COLS)
     vmem = pl.BlockSpec(memory_space=pltpu.VMEM)
     smem = pl.BlockSpec(memory_space=pltpu.SMEM)
-    hbm = pl.BlockSpec(memory_space=pl.ANY)
+    hbm = pl.BlockSpec(memory_space=pltpu.HBM)
     wide = width + LANES
     f32, bf16 = jnp.float32, jnp.bfloat16
     dma = pltpu.SemaphoreType.DMA
@@ -381,13 +407,25 @@
             jax.ShapeDtypeStruct((NQ, width), f32),
             jax.ShapeDtypeStruct((1,), f32),
         ),
-        in_specs=[vmem, vmem, vmem, vmem, vmem, hbm, vmem, hbm, vmem, vmem, hbm, hbm, vmem, vmem, smem, vmem],
+        in_specs=[hbm] * 16,
         out_specs=(vmem, vmem, smem),
         scratch_shapes=[
+            pltpu.VMEM((rows, cols, width), bf16),
+            pltpu.VMEM(depth_weight.shape, f32),
+            pltpu.VMEM((width,), f32),
+            pltpu.VMEM((width,), f32),
+            pltpu.VMEM((width,), f32),
             pltpu.VMEM((width, hid), bf16),
+            pltpu.VMEM((hid,), f32),
             pltpu.VMEM((hid, width), bf16),
-            pltpu.VMEM((width, width), bf16),
-            pltpu.VMEM((width, width), bf16),
+            pltpu.VMEM((width,), f32),
+            pltpu.VMEM((width,), f32),
+            pltpu.VMEM((width, 2 * width), bf16),
+            pltpu.VMEM((NQ, width), bf16),
+            pltpu.VMEM((class_weight.shape[1], width), f32),
+            pltpu.SMEM(tissue.shape, jnp.int32),
+            pltpu.SMEM(slide_label.shape, jnp.int32),
+            pltpu.VMEM((NQ, width), f32),
             pltpu.VMEM((chunks, rows + 6, cols + 16, LANES), f32),
             pltpu.VMEM((chunks, rows, 16, LANES), f32),
             pltpu.VMEM((chunks, rows, 16, LANES), f32),
@@ -398,12 +436,12 @@
             pltpu.VMEM((2, 3, cols, width), bf16),
             pltpu.VMEM((2, rows * 8, width), bf16),
             pltpu.VMEM((4, 32, width), bf16),
-            pltpu.VMEM((NQ, wide), f32),
+            pltpu.VMEM((GROUP, QROWS, wide), f32),
             pltpu.VMEM((GROUP, QROWS, wide), f32),
             pltpu.VMEM((n_far, QROWS, wide), f32),
             pltpu.VMEM((QROWS, wide), f32),
             pltpu.VMEM((GROUP, QROWS, width), f32),
-            dma((4,)),
+            dma((16,)),
             dma((8,)),
             dma((8,)),
             dma((GROUP,)),
@@ -414,13 +452,12 @@
             dma((GROUP,)),
         ],
         compiler_params=pltpu.CompilerParams(
-            collective_id=0, has_side_effects=True, vmem_limit_bytes=40 * 1024 * 1024
+            collective_id=0, has_side_effects=True, vmem_limit_bytes=63 * 1024 * 1024
         ),
     )(
-        features, depth_weight, depth_bias.reshape(1, width), norm_gain.reshape(1, width),
-        norm_bias.reshape(1, width), expand_weight, expand_bias.reshape(1, hid), shrink_weight,
-        shrink_bias.reshape(1, width), layer_scale.reshape(1, width), key_weight, value_weight,
-        queries, class_weight, tissue, slide_label.reshape(1, -1),
+        features, depth_weight, depth_bias, norm_gain, norm_bias, expand_weight, expand_bias,
+        shrink_weight, shrink_bias, layer_scale, key_weight, value_weight, queries, class_weight.T,
+        tissue, slide_label,
     )
     return block, pooled, loss
 

time: 44.2 us -> 31.1 us (0.70); the launches traced: 43.6 us -> 30.9 us
  local copies, waits for them, and re-layouts: 14.7 us -> 3.16 us
  Pallas kernels: 26.5 us -> 25.3 us
    unnamed x21 -> x2, local copies, waits for them, and re-layouts: 10.6 us -> 3.16 us
    reshape x6 -> x0, local copies, waits for them, and re-layouts: 4.12 us -> none  [the longest x1 0.7 us: per_device(): expand_bias.reshape(1, hid)]
    pallas_call x1, Pallas kernels: 26.5 us -> 25.3 us  [per_device(): pl.pallas_call(functools.partial(kernel, n_row, n_col), out_shape=(jax.Sh...]
where the time goes in v2:
time: 31.1 us; the launch traced here: 30.9 us
  Pallas kernels  25.3 us (81%)
  local copies, waits for them, and re-layouts  3.16 us (10%)
  between operations  2.46 us (8%)
    pallas_call x1, Pallas kernels, per_device(): pl.pallas_call(functools.partial(kernel, n_row, n_col), out_shape=(jax.Sh...  25.3 us
    unnamed x2, local copies, waits for them, and re-layouts  3.16 us

profile of v2, /device:TPU:0, one launch (start us, length us, event | category | flops | bytes accessed | tf_op | source)
XLA Modules:
  0.0 30.9 jit_solution(10188198328450281172)
XLA Ops:
  0.6 25.3 %shard_map.175 = (bf16[8,32,384]{2,1,0:T(8,128)(2,1)}, f32[64,384]{1,0:T(8,128)}, f32[1]{0:T(128)}) custom-call(bf16[8,32,384]{2,1,0:T(8,128)(2,1)} %feat_hbm.1, f32[7,7,384]{2,1,0:T(8,128)} %dw_hbm.1, f32[384]{0:T(512)} %db_hbm.1, f32[384]{0:T(512)} %gain_hbm.1, f32[384]{0:T(512)} %nbias_hbm.1, bf16[384,1536]{1,0:T(8,128)(2,1)} %w1_hbm.1, f32[1536]{0:T(1024)} %b1_hbm.1, ...), custom_call_target="tpu_custom_call" | custom-call | tf_op jit(solution)/shard_map/pallas_call | solution.py:403
  26.0 1.6 %copy.22 = bf16[8,32,384]{2,1,0:T(8,128)(2,1)} copy(bf16[8,32,384]{2,1,0:T(8,128)(2,1)} %get-tuple-element.6) | data formatting | bytes 393216
  27.6 1.5 %copy.23 = f32[64,384]{1,0:T(8,128)} copy(f32[64,384]{1,0:T(8,128)} %get-tuple-element.7) | data formatting | bytes 196608

commit v3 on v2

--- a/solution.py
+++ b/solution.py
@@ -248,13 +248,23 @@
     ).astype(jnp.bfloat16)
 
     hid = w1.shape[1]
-    piece = 384
+    piece = 256
     shrunk = jnp.zeros((count, width), jnp.float32)
-    for start in range(0, hid, piece):
+    starts = list(range(0, hid, piece))
+
+    def expand(start):
         part = slice(start, start + piece)
-        expanded = jnp.dot(normed, w1[:, part], preferred_element_type=jnp.float32) + b1[part].reshape(1, piece)
+        wide = jnp.dot(normed, w1[:, part], preferred_element_type=jnp.float32)
+        return wide + b1[part].reshape(1, piece)
+
+    expanded = expand(starts[0])
+    for i, start in enumerate(starts):
+        following = expand(starts[i + 1]) if i + 1 < len(starts) else None
         hidden = (0.5 * expanded * (1.0 + lax.erf(expanded * 0.5**0.5))).astype(jnp.bfloat16)
-        shrunk = shrunk + jnp.dot(hidden, w2[part, :], preferred_element_type=jnp.float32)
+        shrunk = shrunk + jnp.dot(
+            hidden, w2[start : start + piece, :], preferred_element_type=jnp.float32
+        )
+        expanded = following
     shrunk = shrunk + b2[...].reshape(1, width)
     inputs = feat[...].astype(jnp.float32).reshape(count, width)
     block = (inputs + scale[...].reshape(1, width) * shrunk).astype(jnp.bfloat16)
@@ -403,8 +413,8 @@
     block, pooled, loss = pl.pallas_call(
         functools.partial(kernel, n_row, n_col),
         out_shape=(
-            jax.ShapeDtypeStruct((rows, cols, width), bf16),
-            jax.ShapeDtypeStruct((NQ, width), f32),
+            pltpu.VMEM((rows, cols, width), bf16),
+            pltpu.VMEM((NQ, width), f32),
             jax.ShapeDtypeStruct((1,), f32),
         ),
         in_specs=[hbm] * 16,

time: 31.1 us -> 28.6 us (0.920)
  local copies, waits for them, and re-layouts: 3.16 us -> 1.32 us
  Pallas kernels: 25.3 us -> 24.8 us
    unnamed x2, local copies, waits for them, and re-layouts: 3.16 us -> 1.32 us
    pallas_call x1, Pallas kernels: 25.3 us -> 24.8 us  [per_device(): pl.pallas_call(functools.partial(kernel, n_row, n_col), out_shape=(pltpu....]
where the time goes in v3:
time: 28.6 us; the launch traced here: 28.5 us
  Pallas kernels  24.8 us (87%)
  between operations  2.33 us (8%)
  local copies, waits for them, and re-layouts  1.32 us (5%)
    pallas_call x1, Pallas kernels, per_device(): pl.pallas_call(functools.partial(kernel, n_row, n_col), out_shape=(pltpu....  24.8 us
    unnamed x2, local copies, waits for them, and re-layouts  1.32 us

profile of v3, /device:TPU:0, one launch (start us, length us, event | category | flops | bytes accessed | tf_op | source)
XLA Modules:
  0.0 28.5 jit_solution(17732009136395308338)
XLA Ops:
  0.6 24.8 %shard_map.175 = (bf16[8,32,384]{2,1,0:T(8,128)(2,1)S(1)}, f32[64,384]{1,0:T(8,128)S(1)}, f32[1]{0:T(128)}) custom-call(bf16[8,32,384]{2,1,0:T(8,128)(2,1)} %feat_hbm.1, f32[7,7,384]{2,1,0:T(8,128)} %dw_hbm.1, f32[384]{0:T(512)} %db_hbm.1, f32[384]{0:T(512)} %gain_hbm.1, f32[384]{0:T(512)} %nbias_hbm.1, bf16[384,1536]{1,0:T(8,128)(2,1)} %w1_hbm.1, ...), custom_call_target="tpu_custom_call" | custom-call | tf_op jit(solution)/shard_map/pallas_call | solution.py:413
  25.5 0.7 %copy.22 = bf16[8,32,384]{2,1,0:T(8,128)(2,1)} copy(bf16[8,32,384]{2,1,0:T(8,128)(2,1)S(1)} %get-tuple-element.3) | data formatting | bytes 393216
  26.1 0.6 %copy.23 = f32[64,384]{1,0:T(8,128)} copy(f32[64,384]{1,0:T(8,128)S(1)} %get-tuple-element.4) | data formatting | bytes 196608

commit v4 on v3

--- a/solution.py
+++ b/solution.py
@@ -31,6 +31,15 @@
     for h in range(NH):
         out = jnp.where(head == h, cols[:, first + h : first + h + 1], out)
     return out
+
+
+def gelu(x):
+    size = jnp.abs(x)
+    t = 1.0 / (1.0 + (0.3275911 * 0.5**0.5) * size)
+    poly = 0.5 * 1.061405429
+    for term in (-1.453152027, 1.421413741, -0.284496736, 0.254829592):
+        poly = poly * t + 0.5 * term
+    return jnp.maximum(x, 0.0) - size * (poly * t) * jnp.exp(-0.5 * (x * x))
 
 
 def combine(ref, count, width):
@@ -67,8 +76,7 @@
         (label_hbm, label),
     )
     loads = [pltpu.make_async_copy(src, dst, w_sem.at[i]) for i, (src, dst) in enumerate(sources)]
-    for load in loads:
-        load.start()
+    loads[0].start()
 
     base_row, base_col = (row // GROUP_ROWS) * GROUP_ROWS, (col // GROUP_COLS) * GROUP_COLS
     place = (row - base_row) * GROUP_COLS + (col - base_col)
@@ -108,6 +116,8 @@
     for step in range(1, n_far):
         pl.semaphore_signal(barrier, inc=1, device_id=far_peer(step)[1], device_id_type=MESH)
 
+    for load in loads[1:4]:
+        load.start()
     loads[0].wait()
     stage_l[...] = feat[:, 0:8, :].astype(jnp.float32).reshape(rows * 8, width).astype(jnp.bfloat16)
     stage_r[...] = (
@@ -150,6 +160,9 @@
         @pl.when(jnp.logical_not(present(side)))
         def _(side=side):
             landing[side][...] = jnp.zeros(landing[side].shape, jnp.bfloat16)
+
+    for load in loads[4:]:
+        load.start()
 
     for c in range(chunks):
         lanes = slice(c * LANES, (c + 1) * LANES)
@@ -260,7 +273,7 @@
     expanded = expand(starts[0])
     for i, start in enumerate(starts):
         following = expand(starts[i + 1]) if i + 1 < len(starts) else None
-        hidden = (0.5 * expanded * (1.0 + lax.erf(expanded * 0.5**0.5))).astype(jnp.bfloat16)
+        hidden = gelu(expanded).astype(jnp.bfloat16)
         shrunk = shrunk + jnp.dot(
             hidden, w2[start : start + piece, :], preferred_element_type=jnp.float32
         )

time: 28.6 us -> 29.2 us (1.021)
  Pallas kernels: 24.8 us -> 25.4 us
    pallas_call x1, Pallas kernels: 24.8 us -> 25.4 us  [per_device(): pl.pallas_call(functools.partial(kernel, n_row, n_col), out_shape=(pltpu....]
where the time goes in v4:
time: 29.2 us; the launch traced here: 29.1 us
  Pallas kernels  25.4 us (87%)
  between operations  2.33 us (8%)
  local copies, waits for them, and re-layouts  1.32 us (5%)
    pallas_call x1, Pallas kernels, per_device(): pl.pallas_call(functools.partial(kernel, n_row, n_col), out_shape=(pltpu....  25.4 us
    unnamed x2, local copies, waits for them, and re-layouts  1.32 us

profile of v4, /device:TPU:0, one launch (start us, length us, event | category | flops | bytes accessed | tf_op | source)
XLA Modules:
  0.0 29.1 jit_solution(17465196569187795710)
XLA Ops:
  0.6 25.4 %shard_map.175 = (bf16[8,32,384]{2,1,0:T(8,128)(2,1)S(1)}, f32[64,384]{1,0:T(8,128)S(1)}, f32[1]{0:T(128)}) custom-call(bf16[8,32,384]{2,1,0:T(8,128)(2,1)} %feat_hbm.1, f32[7,7,384]{2,1,0:T(8,128)} %dw_hbm.1, f32[384]{0:T(512)} %db_hbm.1, f32[384]{0:T(512)} %gain_hbm.1, f32[384]{0:T(512)} %nbias_hbm.1, bf16[384,1536]{1,0:T(8,128)(2,1)} %w1_hbm.1, ...), custom_call_target="tpu_custom_call" | custom-call | tf_op jit(solution)/shard_map/pallas_call | solution.py:426
  26.1 0.7 %copy.22 = bf16[8,32,384]{2,1,0:T(8,128)(2,1)} copy(bf16[8,32,384]{2,1,0:T(8,128)(2,1)S(1)} %get-tuple-element.3) | data formatting | bytes 393216
  26.8 0.6 %copy.23 = f32[64,384]{1,0:T(8,128)} copy(f32[64,384]{1,0:T(8,128)S(1)} %get-tuple-element.4) | data formatting | bytes 196608

commit v5 on v3

--- a/solution.py
+++ b/solution.py
@@ -67,8 +67,7 @@
         (label_hbm, label),
     )
     loads = [pltpu.make_async_copy(src, dst, w_sem.at[i]) for i, (src, dst) in enumerate(sources)]
-    for load in loads:
-        load.start()
+    loads[0].start()
 
     base_row, base_col = (row // GROUP_ROWS) * GROUP_ROWS, (col // GROUP_COLS) * GROUP_COLS
     place = (row - base_row) * GROUP_COLS + (col - base_col)
@@ -108,6 +107,8 @@
     for step in range(1, n_far):
         pl.semaphore_signal(barrier, inc=1, device_id=far_peer(step)[1], device_id_type=MESH)
 
+    for load in loads[1:]:
+        load.start()
     loads[0].wait()
     stage_l[...] = feat[:, 0:8, :].astype(jnp.float32).reshape(rows * 8, width).astype(jnp.bfloat16)
     stage_r[...] = (

time: 28.6 us -> 28.6 us (level)
  no operation moved by 1% of the time
where the time goes in v5:
time: 28.6 us; the launch traced here: 28.4 us
  Pallas kernels  24.8 us (87%)
  between operations  2.33 us (8%)
  local copies, waits for them, and re-layouts  1.32 us (5%)
    pallas_call x1, Pallas kernels, per_device(): pl.pallas_call(functools.partial(kernel, n_row, n_col), out_shape=(pltpu....  24.8 us
    unnamed x2, local copies, waits for them, and re-layouts  1.32 us

profile of v5, /device:TPU:0, one launch (start us, length us, event | category | flops | bytes accessed | tf_op | source)
XLA Modules:
  0.0 28.4 jit_solution(5878022260899409271)
XLA Ops:
  0.6 24.8 %shard_map.175 = (bf16[8,32,384]{2,1,0:T(8,128)(2,1)S(1)}, f32[64,384]{1,0:T(8,128)S(1)}, f32[1]{0:T(128)}) custom-call(bf16[8,32,384]{2,1,0:T(8,128)(2,1)} %feat_hbm.1, f32[7,7,384]{2,1,0:T(8,128)} %dw_hbm.1, f32[384]{0:T(512)} %db_hbm.1, f32[384]{0:T(512)} %gain_hbm.1, f32[384]{0:T(512)} %nbias_hbm.1, bf16[384,1536]{1,0:T(8,128)(2,1)} %w1_hbm.1, ...), custom_call_target="tpu_custom_call" | custom-call | tf_op jit(solution)/shard_map/pallas_call | solution.py:414
  25.4 0.7 %copy.22 = bf16[8,32,384]{2,1,0:T(8,128)(2,1)} copy(bf16[8,32,384]{2,1,0:T(8,128)(2,1)S(1)} %get-tuple-element.3) | data formatting | bytes 393216
  26.1 0.6 %copy.23 = f32[64,384]{1,0:T(8,128)} copy(f32[64,384]{1,0:T(8,128)S(1)} %get-tuple-element.4) | data formatting | bytes 196608

commit v6 on v5

--- a/solution.py
+++ b/solution.py
@@ -14,7 +14,7 @@
 GROUP_ROWS, GROUP_COLS = 4, 2
 GROUP = GROUP_ROWS * GROUP_COLS
 QROWS = NQ // GROUP
-ORDER = (4, 5, 6, 7, 1, 2, 3, 0)
+ORDER = (7, 5, 6, 4, 3, 1, 2, 0)
 CALLS = 2
 MESH = pl.DeviceIdType.MESH
 SIDES = [(-1, 0), (1, 0), (0, -1), (0, 1), (-1, -1), (-1, 1), (1, -1), (1, 1)]
@@ -76,7 +76,11 @@
     far = (row // GROUP_ROWS) * over + col // GROUP_COLS
 
     def near_peer(step):
-        other = (place + step) % GROUP
+        other = (
+            (place // 4 + step // 4) % 2 * 4
+            + (place // 2 + step // 2) % 2 * 2
+            + (place + step) % 2
+        )
         return other, (base_row + other // GROUP_COLS, base_col + other % GROUP_COLS)
 
     def far_peer(step):
@@ -356,7 +360,7 @@
     pooled[place] = weighted / spread(tail, NH, width)
 
     copies_c = []
-    for step in range(1, GROUP):
+    for step in ORDER[:-1]:
         other, device = near_peer(step)
         copies_c.append(pltpu.make_async_remote_copy(
             src_ref=pooled.at[place],

time: 28.6 us -> 28.6 us (level)
  no operation moved by 1% of the time
where the time goes in v6:
time: 28.6 us; the launch traced here: 28.5 us
  Pallas kernels  24.8 us (87%)
  between operations  2.33 us (8%)
  local copies, waits for them, and re-layouts  1.32 us (5%)
    pallas_call x1, Pallas kernels, per_device(): pl.pallas_call(functools.partial(kernel, n_row, n_col), out_shape=(pltpu....  24.8 us
    unnamed x2, local copies, waits for them, and re-layouts  1.32 us

profile of v6, /device:TPU:0, one launch (start us, length us, event | category | flops | bytes accessed | tf_op | source)
XLA Modules:
  0.0 28.5 jit_solution(3741030720087814656)
XLA Ops:
  0.6 24.8 %shard_map.175 = (bf16[8,32,384]{2,1,0:T(8,128)(2,1)S(1)}, f32[64,384]{1,0:T(8,128)S(1)}, f32[1]{0:T(128)}) custom-call(bf16[8,32,384]{2,1,0:T(8,128)(2,1)} %feat_hbm.1, f32[7,7,384]{2,1,0:T(8,128)} %dw_hbm.1, f32[384]{0:T(512)} %db_hbm.1, f32[384]{0:T(512)} %gain_hbm.1, f32[384]{0:T(512)} %nbias_hbm.1, bf16[384,1536]{1,0:T(8,128)(2,1)} %w1_hbm.1, ...), custom_call_target="tpu_custom_call" | custom-call | tf_op jit(solution)/shard_map/pallas_call | solution.py:418
  25.5 0.7 %copy.22 = bf16[8,32,384]{2,1,0:T(8,128)(2,1)} copy(bf16[8,32,384]{2,1,0:T(8,128)(2,1)S(1)} %get-tuple-element.3) | data formatting | bytes 393216
  26.1 0.6 %copy.23 = f32[64,384]{1,0:T(8,128)} copy(f32[64,384]{1,0:T(8,128)S(1)} %get-tuple-element.4) | data formatting | bytes 196608

commit v7 on v6

--- a/solution.py
+++ b/solution.py
@@ -15,7 +15,7 @@
 GROUP = GROUP_ROWS * GROUP_COLS
 QROWS = NQ // GROUP
 ORDER = (7, 5, 6, 4, 3, 1, 2, 0)
-CALLS = 2
+CALLS = 1
 MESH = pl.DeviceIdType.MESH
 SIDES = [(-1, 0), (1, 0), (0, -1), (0, 1), (-1, -1), (-1, 1), (1, -1), (1, 1)]
 
@@ -254,7 +254,7 @@
 
     hid = w1.shape[1]
     piece = 256
-    shrunk = jnp.zeros((count, width), jnp.float32)
+    hiddens = []
     starts = list(range(0, hid, piece))
 
     def expand(start):
@@ -266,10 +266,9 @@
     for i, start in enumerate(starts):
         following = expand(starts[i + 1]) if i + 1 < len(starts) else None
         hidden = (0.5 * expanded * (1.0 + lax.erf(expanded * 0.5**0.5))).astype(jnp.bfloat16)
-        shrunk = shrunk + jnp.dot(
-            hidden, w2[start : start + piece, :], preferred_element_type=jnp.float32
-        )
+        hiddens.append(hidden)
         expanded = following
+    shrunk = jnp.dot(jnp.concatenate(hiddens, axis=1), w2[...], preferred_element_type=jnp.float32)
     shrunk = shrunk + b2[...].reshape(1, width)
     inputs = feat[...].astype(jnp.float32).reshape(count, width)
     block = (inputs + scale[...].reshape(1, width) * shrunk).astype(jnp.bfloat16)

time: 28.6 us -> 28.9 us (1.010)
  Pallas kernels: 24.8 us -> 25.1 us
where the time goes in v7:
time: 28.9 us; the launch traced here: 28.7 us
  Pallas kernels  25.1 us (87%)
  between operations  2.33 us (8%)
  local copies, waits for them, and re-layouts  1.32 us (5%)
    pallas_call x1, Pallas kernels, per_device(): pl.pallas_call(functools.partial(kernel, n_row, n_col), out_shape=(pltpu....  25.1 us
    unnamed x2, local copies, waits for them, and re-layouts  1.32 us

profile of v7, /device:TPU:0, one launch (start us, length us, event | category | flops | bytes accessed | tf_op | source)
XLA Modules:
  0.0 28.7 jit_solution(17753913026970649521)
XLA Ops:
  0.6 25.1 %shard_map.175 = (bf16[8,32,384]{2,1,0:T(8,128)(2,1)S(1)}, f32[64,384]{1,0:T(8,128)S(1)}, f32[1]{0:T(128)}) custom-call(bf16[8,32,384]{2,1,0:T(8,128)(2,1)} %feat_hbm.1, f32[7,7,384]{2,1,0:T(8,128)} %dw_hbm.1, f32[384]{0:T(512)} %db_hbm.1, f32[384]{0:T(512)} %gain_hbm.1, f32[384]{0:T(512)} %nbias_hbm.1, bf16[384,1536]{1,0:T(8,128)(2,1)} %w1_hbm.1, ...), custom_call_target="tpu_custom_call" | custom-call | tf_op jit(solution)/shard_map/pallas_call | solution.py:417
  25.7 0.7 %copy.22 = bf16[8,32,384]{2,1,0:T(8,128)(2,1)} copy(bf16[8,32,384]{2,1,0:T(8,128)(2,1)S(1)} %get-tuple-element.3) | data formatting | bytes 393216
  26.4 0.6 %copy.23 = f32[64,384]{1,0:T(8,128)} copy(f32[64,384]{1,0:T(8,128)S(1)} %get-tuple-element.4) | data formatting | bytes 196608
